TPU v7x, 128 devices: a whole 4x4x4 slice. The times are simulated.
128 devices in a mesh: replica: 4 (over z_lo, core), fsdp: 32 (over x, y, z_hi).
Axes of the slice: x: 4, y: 4, z: 4 (z_hi: 2, z_lo: 2; z = z_hi * 2 + z_lo), core: 2. Of those that a mesh axis runs over, the one named last changes fastest.
Arguments:
- levels: int32 [4, 8192, 8192], P('replica', 'fsdp'), may hold values from -8 to 7
- scales: float32 [4, 8192, 64], P('replica', 'fsdp'), may hold values from 0.02 to 0.2
- master: float32 [8192, 8192], P('replica', 'fsdp'), may hold values from -6 to 6
- momentum: float32 [8192, 8192], P('replica', 'fsdp'), may hold values from -4 to 4
Outputs:
- new_master: float32 [8192, 8192], P('replica', 'fsdp')
- new_momentum: float32 [8192, 8192], P('replica', 'fsdp')
- weights: bfloat16 [8192, 8192], P('fsdp')
All inputs are finite; a program needn't handle non-finite values.
Results may differ from a plain program's by a relative error of at most 0.007.
Values may be sent and summed in bfloat16 or wider, within the bound.
A program may use at most 128 MiB of HBM per device.

v0:
```python
import jax
import jax.numpy as jnp
from jax import lax
from jax.sharding import PartitionSpec as P

BLOCK = 128


outer_rate = 0.7
momentum_coef = 0.9


def per_device(levels, scales, master, momentum):
    row_count = levels.shape[1]
    column_count = levels.shape[2]
    blocks = levels[0].astype(jnp.float32).reshape(row_count, column_count // BLOCK, BLOCK)
    decoded = (blocks * scales[0][:, :, None]).reshape(row_count, column_count).astype(jnp.bfloat16)
    replicas = lax.axis_size("replica")
    columns = lax.all_to_all(decoded, "fsdp", split_axis=1, concat_axis=0, tiled=True)
    summed = lax.psum_scatter(
        columns.astype(jnp.float32).astype(jnp.bfloat16), "replica", scatter_dimension=0, tiled=True
    ).astype(jnp.float32)
    outer_grad = summed / replicas
    new_momentum = momentum_coef * momentum + outer_grad
    new_master = master - outer_rate * (outer_grad + momentum_coef * new_momentum)
    new_weights = new_master.astype(jnp.bfloat16)
    full_rows = lax.all_gather(new_weights, "replica", axis=0, tiled=True)
    own_rows = lax.all_to_all(full_rows, "fsdp", split_axis=0, concat_axis=1, tiled=True)
    return (new_master, new_momentum, own_rows)


def solution(mesh):
    in_specs = (
        P("replica", "fsdp", None),
        P("replica", "fsdp", None),
        P("replica", "fsdp"),
        P("replica", "fsdp"),
    )
    out_specs = (P("replica", "fsdp"), P("replica", "fsdp"), P("fsdp", None))
    return jax.shard_map(
        per_device, mesh=mesh, in_specs=in_specs, out_specs=out_specs, check_vma=False
    )
```

profile of v0, /device:TPU:1, one launch (start us, length us, event | category | flops | bytes accessed | tf_op | source)
XLA Modules:
  0.0 270.9 jit_solution(1578497498592604480)
XLA Ops:
  7.2 0.0 reduce-scatter.2.cloned.1.call-start
  7.2 7.5 %convert_element_type.21 = f32[1,256,8192]{2,1,0:T(8,128)} convert(s32[1,256,8192]{2,1,0:T(8,128)} %param.4) | non-fusion elementwise | flops 2097152 | bytes 16777216 | tf_op jit(solution)/shard_map/convert_element_type | solution.py:16
  14.7 0.0 copy-start.1
  14.7 9.0 %copy.12 = f32[1,256,8192]{1,2,0:T(8,128)} copy(f32[1,256,8192]{2,1,0:T(8,128)} %convert_element_type.21) | data formatting | bytes 16777216 | tf_op jit(solution)/shard_map/convert_element_type | solution.py:16
  23.7 0.0 copy-done.1
  23.7 3.9 %mul.27 = f32[256,64,128]{0,2,1:T(8,128)} broadcast(f32[256,64]{0,1:T(8,128)S(1)} %bitcast.20), dimensions={0,1} | broadcast | bytes 8454144 | tf_op jit(solution)/shard_map/mul | solution.py:17
  27.6 7.1 %fusion = bf16[256,32,256]{0,2,1:T(8,128)(2,1)S(1)} fusion(f32[256,32,256]{0,2,1:T(8,128)} %bitcast.13, f32[256,32,256]{0,2,1:T(8,128)} %bitcast.14), kind=kLoop, calls=%fused_computation.1 | loop fusion | flops 4194304 | bytes 20971520 | tf_op jit(solution)/shard_map/convert_element_type | solution.py:17
  34.7 62.4 %all_to_all.35 = bf16[256,32,256]{0,2,1:T(8,128)(2,1)} all-to-all(bf16[256,32,256]{0,2,1:T(8,128)(2,1)S(1)} %fusion), channel_id=1, replica_groups=mesh['replica'=4,'fsdp'=32] {'fsdp'}, dimensions={1} | all-to-all | bytes 8388608 | tf_op jit(solution)/shard_map/all_to_all | solution.py:19
  97.1 6.4 %copy.13 = bf16[32,256,256]{2,1,0:T(8,128)(2,1)} copy(bf16[32,256,256]{1,2,0:T(8,128)(2,1)} %bitcast.16) | data formatting | bytes 8388608 | tf_op jit(solution)/shard_map/all_to_all | solution.py:19
  103.5 0.0 copy-start
  103.5 0.0 reduce-scatter.2.cloned.1.call-update
  103.6 0.0 all-gather.2.cloned.1.call-start
  103.6 43.4 %reduce-scatter.2.cloned.1.call-done = bf16[2048,256]{1,0:T(8,128)(2,1)} async-done(((bf16[8192,256]{1,0:T(8,128)(2,1)}), bf16[2048,256]{1,0:T(8,128)(2,1)}) %reduce-scatter.2.cloned.1.call-update) | async-done | bytes 1048592 | tf_op jit(solution)/shard_map/reduce_scatter | solution.py:20
  147.0 0.0 copy-done
  147.0 4.9 %fusion.1 = (bf16[2048,256]{1,0:T(8,128)(2,1)}, f32[2048,256]{1,0:T(8,128)}, f32[2048,256]{1,0:T(8,128)}) fusion(f32[2048,256]{1,0:T(8,128)S(1)} %copy-done, bf16[2048,256]{1,0:T(8,128)(2,1)} %reduce-scatter.2.cloned.1.call-done, f32[2048,256]{1,0:T(8,128)} %param.7), kind=kLoop, calls=%fused_computation.5 | loop fusion | flops 4718592 | bytes 10485760 | tf_op jit(solution)/shard_map/convert_element_type | solution.py:26
  151.9 0.0 all-gather.2.cloned.1.call-update
  151.9 47.9 %all-gather.2.cloned.1.call-done = bf16[8192,256]{1,0:T(8,128)(2,1)} async-done(((bf16[2048,256]{1,0:T(8,128)(2,1)}), bf16[8192,256]{1,0:T(8,128)(2,1)}) %all-gather.2.cloned.1.call-update) | async-done | bytes 4194320 | tf_op jit(solution)/shard_map/all_gather | solution.py:27
  199.8 61.7 %all_to_all.36 = bf16[32,256,256]{2,1,0:T(8,128)(2,1)S(1)} all-to-all(bf16[32,256,256]{2,1,0:T(8,128)(2,1)} %bitcast.18), channel_id=1, replica_groups=mesh['replica'=4,'fsdp'=32] {'fsdp'}, dimensions={0} | all-to-all | bytes 8388608 | tf_op jit(solution)/shard_map/all_to_all | solution.py:28
  261.5 2.5 copy.15
Async XLA Ops:
  7.2 139.9 %reduce-scatter.2.cloned.1.call-start = ((), (), s32[]{:S(2)}) async-start(), calls=%async_computation.3 | async-start | bytes 5242880 | tf_op jit(solution)/shard_map/reduce_scatter | solution.py:20
  14.7 9.0 %copy-start.1 = (f32[1,256,64]{1,2,0:T(8,128)S(1)}, f32[1,256,64]{1,2,0:T(8,128)}, u32[]{:S(2)}) copy-start(f32[1,256,64]{1,2,0:T(8,128)} %param.5) | copy-start | bytes 196612
  103.5 43.5 %copy-start = (f32[2048,256]{1,0:T(8,128)S(1)}, f32[2048,256]{1,0:T(8,128)}, u32[]{:S(2)}) copy-start(f32[2048,256]{1,0:T(8,128)} %param.6) | copy-start | bytes 6291460
  103.6 96.3 %all-gather.2.cloned.1.call-start = ((), (), s32[]{:S(2)}) async-start(), calls=%async_computation.4 | async-start | bytes 5242880 | tf_op jit(solution)/shard_map/all_gather | solution.py:27
Sparse Core Ops, SparseCore 0:
  103.7 43.2 reduce-scatter.1
  152.1 47.7 all-gather.1
where the time goes:
time: 271 us
  blocking collectives  124 us (46%)
  waiting for transfers between devices  91.3 us (34%)
  local copies, waits for them, and re-layouts  21.9 us (8%)
  other arithmetic  19.5 us (7%)
  between operations  14 us (5%)
    all_to_all x1, blocking collectives, per_device(): lax.all_to_all(decoded, 'fsdp', split_axis=1, concat_axis=0, tiled=True)  62.4 us
    all_to_all x1, blocking collectives, per_device(): lax.all_to_all(full_rows, 'fsdp', split_axis=0, concat_axis=1, tiled=True)  61.7 us
    all_gather x1, waiting for transfers between devices, per_device(): full_rows = lax.all_gather(new_weights, 'replica', axis=0, tiled=True)  47.9 us
    reduce_scatter x1, waiting for transfers between devices, per_device(): lax.psum_scatter(columns.astype(jnp.float32).astype(jnp.bfloat16), 'repli...  43.4 us
    convert_element_type x1, local copies, waits for them, and re-layouts, per_device(): levels[0].astype(jnp.float32)  9.04 us
    convert_element_type x1, other arithmetic, per_device(): levels[0].astype(jnp.float32)  7.49 us
    convert_element_type x1, other arithmetic, per_device(): (blocks * scales[0][:, :, None]).reshape(row_count, column_count)  7.11 us
    all_to_all x1, local copies, waits for them, and re-layouts, per_device(): lax.all_to_all(decoded, 'fsdp', split_axis=1, concat_axis=0, tiled=True)  6.4 us
  transfers between devices with their start and end apart: 2, of which 2 were waited for; matrix products, arithmetic and copies ran while one was open for 0% of the time, Pallas kernels for 0%

commit v1 on v0

v1 whole, which is shorter than its diff:
```python
import functools

import jax
import jax.numpy as jnp
from jax import lax
from jax.experimental import pallas as pl
from jax.experimental.pallas import tpu as pltpu
from jax.sharding import PartitionSpec as P

MESH = pl.DeviceIdType.MESH
F32 = jnp.float32
BF16 = jnp.bfloat16

BLOCK = 128
ROWS = 128
COLS = 256
CHUNKS = 16
LOADS = 8

outer_rate = 0.7
momentum_coef = 0.9
MOM = outer_rate * momentum_coef * momentum_coef
GRAD = outer_rate * (1.0 + momentum_coef)


def kernel(
    levels, scales, master, momentum,
    out_master, out_momentum, out_w,
    lv, sc, mas, mom, dec, crec, zbuf, zrec, gbuf, grec, ubuf, urec, wbuf, wrec,
    lsem, ssem, msem, css, crs, zss, zrs, gss, grs, uss, urs, wzs, wzr, wcs, wcr, wfs, wfr, wls, wms, osem,
):
    r = lax.axis_index("replica")
    f = lax.axis_index("fsdp")
    x, y, zh = f // 8, (f // 2) % 4, f % 2
    zl, c = r // 2, r % 2
    core = (zl * 2 + (1 - c), f)
    zp = ((1 - zl) * 2 + c, f)
    own = (zl + zh + x // 2) % 2
    same = r == x
    my_slot = (y * 2 + zh) * 2 + c
    my_chunk = x * 4 + y

    def chunk(j):
        return ((x + j // 4) % 4) * 4 + (y + j % 4) % 4

    def sum_owner(j):
        return (x, chunk(j) * 2 + own)

    def row_slot(j):
        return (((y + 4 - j // 4) % 4) * 2 + (zh + j // 2) % 2) * 2 + (c + j) % 2

    def row_owner(j):
        zs = (zh + j // 2) % 2
        return (2 * ((zh + zs + zl) % 2) + (c + j) % 2, r * 8 + ((y + 4 - j // 4) % 4) * 2 + zs)

    bar = pltpu.get_barrier_semaphore()
    pl.semaphore_signal(bar, inc=1, device_id=core, device_id_type=MESH)
    pl.semaphore_signal(bar, inc=1, device_id=zp, device_id_type=MESH)

    def greet(j, _):
        @pl.when(jnp.logical_not(same & (j == 0)))
        def _():
            pl.semaphore_signal(bar, inc=1, device_id=sum_owner(j), device_id_type=MESH)
            pl.semaphore_signal(bar, inc=1, device_id=row_owner(j), device_id_type=MESH)
        return 0

    lax.fori_loop(0, 16, greet, 0)

    def load_scales():
        return pltpu.make_async_copy(scales.at[0], sc, ssem)

    def load_levels(i):
        return pltpu.make_async_copy(levels.at[0, :, pl.ds(i * 1024, 1024)], lv.at[i], lsem.at[i])

    def load_master():
        return pltpu.make_async_copy(master, mas, msem.at[0])

    def load_momentum():
        return pltpu.make_async_copy(momentum, mom, msem.at[1])

    load_scales().start()
    for i in range(LOADS):
        load_levels(i).start()
    load_master().start()
    load_momentum().start()

    load_scales().wait()
    for i in range(LOADS):
        load_levels(i).wait()
        for b in range(4):
            block = i * 4 + b
            for h in range(2):
                at = b * COLS + h * BLOCK
                s = sc[:, 2 * block + h:2 * block + h + 1]
                dec[block, :, h * BLOCK:(h + 1) * BLOCK] = (lv[i, :, at:at + BLOCK].astype(F32) * s).astype(BF16)

    load_master().wait()
    load_momentum().wait()

    def make_u(j, _):
        rows = pl.ds(pl.multiple_of(j * ROWS, ROWS), ROWS)
        ubuf[j] = (mas[rows, :] - MOM * mom[rows, :]).astype(BF16)
        return 0

    lax.fori_loop(0, 16, make_u, 0)

    pl.semaphore_wait(bar, 34 - 2 * same.astype(jnp.int32))

    def remote(src, dst, send, recv, device):
        return pltpu.make_async_remote_copy(
            src_ref=src, dst_ref=dst, send_sem=send, recv_sem=recv, device_id=device, device_id_type=MESH
        )

    mine = pl.ds(pl.multiple_of(c * ROWS, ROWS), ROWS)
    others = pl.ds(pl.multiple_of((1 - c) * ROWS, ROWS), ROWS)

    def core_copy(k):
        return remote(dec.at[pl.ds(2 * k, 2), others, :], crec.at[pl.ds(2 * k, 2)], css.at[k], crs.at[k], core)

    def z_copy(k):
        return remote(zbuf.at[k], zrec.at[k], zss.at[k], zrs.at[k], zp)

    def u_copy(j):
        return remote(ubuf.at[row_slot(j)], urec.at[my_chunk], uss.at[row_slot(j)], urs.at[my_chunk], row_owner(j))

    def u_wait(k):
        return remote(ubuf.at[0], urec.at[k], uss.at[0], urs.at[k], core)

    def g_copy(j):
        return remote(gbuf.at[chunk(j)], grec.at[my_slot], gss.at[chunk(j)], grs.at[my_slot], sum_owner(j))

    def g_wait(s):
        return remote(gbuf.at[0], grec.at[s], gss.at[0], grs.at[s], core)

    def columns(block):
        return pl.ds(pl.multiple_of(block * COLS, COLS), COLS)

    def w_z(k):
        return remote(wbuf.at[k], wrec.at[k], wzs.at[k], wzr.at[k], zp)

    def w_core(k):
        return remote(wbuf.at[k], out_w.at[mine, columns(2 * k + own)], wcs.at[k], wcr.at[k], core)

    def w_local(k):
        return pltpu.make_async_copy(wbuf.at[k], out_w.at[mine, columns(2 * k + own)], wls.at[k])

    def w_forward(k):
        return remote(wrec.at[k], out_w.at[mine, columns(2 * k + 1 - own)], wfs.at[k], wfr.at[k], core)

    def w_keep(k):
        return pltpu.make_async_copy(wrec.at[k], out_w.at[mine, columns(2 * k + 1 - own)], wms.at[k])

    def w_core_wait(k):
        return remote(wbuf.at[k], out_w.at[others, columns(2 * k + own)], wcs.at[k], wcr.at[k], core)

    def w_forward_wait(k):
        return remote(wrec.at[k], out_w.at[others, columns(2 * k + 1 - own)], wfs.at[k], wfr.at[k], core)

    def slot_rows(s):
        return pl.ds(pl.multiple_of(s * ROWS, ROWS), ROWS)

    def put_momentum(s):
        return pltpu.make_async_copy(mom.at[slot_rows(s)], out_momentum.at[slot_rows(s)], osem.at[0, s])

    def put_master(s):
        return pltpu.make_async_copy(mas.at[slot_rows(s)], out_master.at[slot_rows(s)], osem.at[1, s])

    def send_core(j, _):
        core_copy(chunk(j)).start()
        return 0

    lax.fori_loop(0, 16, send_core, 0)

    def send_u(j, _):
        here = same & (j == 0)

        @pl.when(here)
        def _():
            urec[my_chunk] = ubuf[my_slot]

        @pl.when(jnp.logical_not(here))
        def _():
            u_copy(j).start()
        return 0

    def send_z(j, _):
        k = chunk(j)
        b = 2 * k + 1 - own
        core_copy(k).wait_recv()
        zbuf[k] = (dec[b, mine, :].astype(F32) + crec[b].astype(F32)).astype(BF16)
        z_copy(k).start()
        return 0

    lax.fori_loop(0, 4, send_z, 0)
    lax.fori_loop(0, 16, send_u, 0)
    lax.fori_loop(4, 16, send_z, 0)

    def whole(j, _):
        k = chunk(j)
        b = 2 * k + own
        here = same & (j == 0)
        z_copy(k).wait_recv()
        gbuf[k] = (dec[b, mine, :].astype(F32) + crec[b].astype(F32) + zrec[k].astype(F32)).astype(BF16)

        @pl.when(here)
        def _():
            grec[my_slot] = gbuf[k]

        @pl.when(jnp.logical_not(here))
        def _():
            g_copy(j).start()
            u_wait(k).wait_recv()

        total = dec[b, mine, :].astype(F32) + crec[b].astype(F32) + zrec[k].astype(F32)
        wbuf[k] = (urec[k].astype(F32) - (GRAD / 4) * total).astype(BF16)
        w_z(k).start()
        w_core(k).start()
        w_local(k).start()
        return 0

    lax.fori_loop(0, 16, whole, 0)

    def update(j, _):
        s = row_slot(j)
        rows = slot_rows(s)

        @pl.when(jnp.logical_not(same & (j == 0)))
        def _():
            g_wait(s).wait_recv()

        g = grec[s].astype(F32) * 0.25
        new_momentum = momentum_coef * mom[rows, :] + g
        mom[rows, :] = new_momentum
        mas[rows, :] = mas[rows, :] - outer_rate * (g + momentum_coef * new_momentum)
        put_momentum(s).start()
        put_master(s).start()
        return 0

    lax.fori_loop(0, 16, update, 0)

    def pass_on(j, _):
        k = chunk(j)
        w_z(k).wait_recv()
        w_forward(k).start()
        w_keep(k).start()
        return 0

    lax.fori_loop(0, 16, pass_on, 0)

    def finish(j, _):
        k = chunk(j)
        core_copy(k).wait_send()
        z_copy(k).wait_send()

        @pl.when(jnp.logical_not(same & (j == 0)))
        def _():
            u_copy(j).wait_send()
            g_copy(j).wait_send()

        put_momentum(j).wait()
        put_master(j).wait()
        w_z(k).wait_send()
        w_core(k).wait_send()
        w_local(k).wait()
        w_core_wait(k).wait_recv()
        w_forward(k).wait_send()
        w_keep(k).wait()
        w_forward_wait(k).wait_recv()
        return 0

    lax.fori_loop(0, 16, finish, 0)


def per_device(levels, scales, master, momentum):
    small = pltpu.VMEM((CHUNKS, ROWS, COLS), BF16)
    sems = pltpu.SemaphoreType.DMA((16,))
    hbm = pl.BlockSpec(memory_space=pl.ANY)
    return pl.pallas_call(
        kernel,
        out_shape=(
            jax.ShapeDtypeStruct(master.shape, F32),
            jax.ShapeDtypeStruct(momentum.shape, F32),
            jax.ShapeDtypeStruct(levels.shape[1:], BF16),
        ),
        in_specs=[hbm] * 4,
        out_specs=(hbm,) * 3,
        scratch_shapes=[
            pltpu.VMEM((LOADS, 2 * ROWS, 1024), jnp.int32),
            pltpu.VMEM((2 * ROWS, 64), F32),
            pltpu.VMEM(master.shape, F32),
            pltpu.VMEM(momentum.shape, F32),
            pltpu.VMEM((2 * CHUNKS, 2 * ROWS, COLS), BF16),
            pltpu.VMEM((2 * CHUNKS, ROWS, COLS), BF16),
        ]
        + [small] * 8
        + [
            pltpu.SemaphoreType.DMA((LOADS,)),
            pltpu.SemaphoreType.DMA,
            pltpu.SemaphoreType.DMA((2,)),
        ]
        + [sems] * 16
        + [pltpu.SemaphoreType.DMA((2, 16))],
        compiler_params=pltpu.CompilerParams(
            collective_id=0, has_side_effects=True, vmem_limit_bytes=40 * 2**20
        ),
    )(levels, scales, master, momentum)


def solution(mesh):
    in_specs = (
        P("replica", "fsdp", None),
        P("replica", "fsdp", None),
        P("replica", "fsdp"),
        P("replica", "fsdp"),
    )
    out_specs = (P("replica", "fsdp"), P("replica", "fsdp"), P("fsdp", None))
    return jax.shard_map(
        per_device, mesh=mesh, in_specs=in_specs, out_specs=out_specs, check_vma=False
    )
```

time: 271 us -> 78.1 us (0.29)
  the two profiles are of different devices: /device:TPU:1 before, /device:TPU:65 now
where the time goes in v1:
time: 78.1 us; the launch traced here: 77.9 us
  Pallas kernels  68.5 us (88%)
  local copies, waits for them, and re-layouts  8.76 us (11%)
    pallas_call x1, Pallas kernels, per_device(): pl.pallas_call(kernel, out_shape=(jax.ShapeDtypeStruct(master.shape, F32)...  68.5 us
    unnamed x8, local copies, waits for them, and re-layouts  8.76 us

profile of v1, /device:TPU:65, one launch (start us, length us, event | category | flops | bytes accessed | tf_op | source)
XLA Modules:
  0.0 77.9 jit_solution(11286742967686981165)
XLA Ops:
  0.6 0.9 %copy.7.scales = f32[1,256,64]{2,1,0:T(8,128)S(1)} copy(f32[1,256,64]{1,2,0:T(8,128)} %param.5) | data formatting | bytes 131072 | tf_op args[1]
  1.6 0.0 copy-start
  1.6 1.6 %copy-done = f32[2048,256]{1,0:T(8,128)S(1)} copy-done((f32[2048,256]{1,0:T(8,128)S(1)}, f32[2048,256]{1,0:T(8,128)}, u32[]{:S(2)}) %copy-start) | copy-done | bytes 2097176
  3.2 0.0 copy-start.1
  3.2 1.6 %copy-done.1 = f32[2048,256]{1,0:T(8,128)S(1)} copy-done((f32[2048,256]{1,0:T(8,128)S(1)}, f32[2048,256]{1,0:T(8,128)}, u32[]{:S(2)}) %copy-start.1) | copy-done | bytes 2097176
  4.8 68.5 %shard_map.67 = (f32[2048,256]{1,0:T(8,128)S(1)}, f32[2048,256]{1,0:T(8,128)S(1)}, bf16[256,8192]{1,0:T(8,128)(2,1)S(1)}) custom-call(s32[1,256,8192]{2,1,0:T(8,128)} %levels.1, f32[1,256,64]{2,1,0:T(8,128)S(1)} %copy.7.scales, f32[2048,256]{1,0:T(8,128)S(1)} %copy-done, f32[2048,256]{1,0:T(8,128)S(1)} %copy-done.1), custom_call_target="tpu_custom_call" | custom-call | tf_op jit(solution)/shard_map/pallas_call | solution.py:278
  73.2 1.3 %copy.11 = f32[2048,256]{1,0:T(8,128)} copy(f32[2048,256]{1,0:T(8,128)S(1)} %get-tuple-element.6) | data formatting | bytes 4194304
  74.5 1.3 %copy.12 = f32[2048,256]{1,0:T(8,128)} copy(f32[2048,256]{1,0:T(8,128)S(1)} %get-tuple-element.7) | data formatting | bytes 4194304
  75.9 2.0 %copy.13 = bf16[256,8192]{1,0:T(8,128)(2,1)} copy(bf16[256,8192]{1,0:T(8,128)(2,1)S(1)} %get-tuple-element.8) | data formatting | bytes 8388608
Async XLA Ops:
  1.6 1.6 %copy-start = (f32[2048,256]{1,0:T(8,128)S(1)}, f32[2048,256]{1,0:T(8,128)}, u32[]{:S(2)}) copy-start(f32[2048,256]{1,0:T(8,128)} %master.1) | copy-start | bytes 6291460
  3.2 1.6 %copy-start.1 = (f32[2048,256]{1,0:T(8,128)S(1)}, f32[2048,256]{1,0:T(8,128)}, u32[]{:S(2)}) copy-start(f32[2048,256]{1,0:T(8,128)} %momentum.1) | copy-start | bytes 6291460

commit v2 on v1

v2 whole, which is shorter than its diff:
```python
import functools

import jax
import jax.numpy as jnp
from jax import lax
from jax.experimental import pallas as pl
from jax.experimental.pallas import tpu as pltpu
from jax.sharding import PartitionSpec as P

MESH = pl.DeviceIdType.MESH
F32 = jnp.float32
BF16 = jnp.bfloat16

BLOCK = 128
ROWS = 128
COLS = 256
CHUNKS = 16
LAG = 3

outer_rate = 0.7
momentum_coef = 0.9
MOM = outer_rate * momentum_coef * momentum_coef
GRAD = outer_rate * (1.0 + momentum_coef)


def kernel(
    levels, scales, master, momentum,
    out_master, out_momentum, out_w,
    lv, sc, sc2, mas, mom, dec, crec, zbuf, zrec, gbuf, grec, ubuf, urec, rel, wbuf, wrec,
    near, far, lsem, ssem, msem, css, crs, zss, zrs, gss, grs, uss, urs, rss, rrs, fss,
    wzs, wzr, wcs, wcr, wfs, wfr, wls, wms, osem,
):
    r = lax.axis_index("replica")
    f = lax.axis_index("fsdp")
    x, y, zh = f // 8, (f // 2) % 4, f % 2
    zl, c = r // 2, r % 2
    core = (zl * 2 + (1 - c), f)
    zp = ((1 - zl) * 2 + c, f)
    cross = (2 * (1 - zl) + c, x * 8 + y * 2 + 1 - zh)
    own = (zl + zh + x // 2) % 2
    same = r == x
    xf = 2 * (1 - zl) + c
    passed = xf == x
    my_slot = (y * 2 + zh) * 2 + c
    my_chunk = x * 4 + y
    leader = r == 0
    herald = r == 3

    def chunk(j):
        b = j % 4
        return ((x + b) % 4) * 4 + (y + j // 4 + b) % 4

    def row_y(i, x_rows):
        return (y + 8 - (x + 4 - x_rows) % 4 - i) % 4

    def row_slot(j):
        return (row_y(j // 4, r) * 2 + (zh + j // 2) % 2) * 2 + (c + j) % 2

    bar = pltpu.get_barrier_semaphore()

    @pl.when(jnp.logical_not(leader))
    def _():
        pl.semaphore_signal(bar, inc=1, device_id=(0, f), device_id_type=MESH)

    def load_scales():
        return pltpu.make_async_copy(scales.at[0], sc, ssem)

    def load_levels(j):
        cols = pl.ds(pl.multiple_of(chunk(j) * 2 * COLS, 2 * COLS), 2 * COLS)
        return pltpu.make_async_copy(levels.at[0, :, cols], lv.at[j], lsem.at[j])

    def load_master():
        return pltpu.make_async_copy(master, mas, msem.at[0])

    def load_momentum():
        return pltpu.make_async_copy(momentum, mom, msem.at[1])

    load_scales().start()

    def load(j, _):
        load_levels(j).start()
        return 0

    lax.fori_loop(0, 16, load, 0)
    load_master().start()
    load_momentum().start()

    @pl.when(leader)
    def _():
        pl.semaphore_wait(bar, 3)
        for member in (1, 2, 3):
            pl.semaphore_signal(near, inc=1, device_id=(member, f), device_id_type=MESH)

    load_scales().wait()
    by_row = jnp.transpose(sc[...])
    sc2[:, :64] = by_row
    sc2[:, 64:] = by_row

    def remote(src, dst, send, recv, device):
        return pltpu.make_async_remote_copy(
            src_ref=src, dst_ref=dst, send_sem=send, recv_sem=recv, device_id=device, device_id_type=MESH
        )

    mine = pl.ds(pl.multiple_of(c * ROWS, ROWS), ROWS)
    others = pl.ds(pl.multiple_of((1 - c) * ROWS, ROWS), ROWS)

    def core_copy(k):
        return remote(dec.at[pl.ds(2 * k, 2), others, :], crec.at[pl.ds(2 * k, 2)], css.at[k], crs.at[k], core)

    def z_copy(k):
        return remote(zbuf.at[k], zrec.at[k], zss.at[k], zrs.at[k], zp)

    def u_copy(i):
        ys, cs = row_y(i // 2, r), (c + i) % 2
        s = (ys * 2 + zh) * 2 + cs
        return remote(ubuf.at[s], urec.at[my_chunk], uss.at[i], urs.at[my_chunk], (2 * zl + cs, r * 8 + ys * 2 + zh))

    def relay_copy(i):
        ys = row_y(i, r)
        return remote(ubuf.at[pl.ds((ys * 2 + 1 - zh) * 2, 2)], rel.at[ys], rss.at[i], rrs.at[ys], cross)

    def relay_wait(i):
        ys = row_y(i, xf)
        return remote(ubuf.at[pl.ds(0, 2)], rel.at[ys], rss.at[i], rrs.at[ys], cross)

    def forward_copy(i):
        ys, cs = row_y(i // 2, xf), (c + i) % 2
        return remote(
            rel.at[ys, cs], urec.at[my_chunk], fss.at[i], urs.at[my_chunk], (2 * zl + cs, xf * 8 + ys * 2 + zh)
        )

    def u_wait(k):
        return remote(ubuf.at[0], urec.at[k], uss.at[0], urs.at[k], core)

    def g_copy(j):
        k = chunk(j)
        return remote(gbuf.at[k], grec.at[my_slot], gss.at[k], grs.at[my_slot], (x, k * 2 + own))

    def g_wait(s):
        return remote(gbuf.at[0], grec.at[s], gss.at[0], grs.at[s], core)

    def columns(block):
        return pl.ds(pl.multiple_of(block * COLS, COLS), COLS)

    def w_z(k):
        return remote(wbuf.at[k], wrec.at[k], wzs.at[k], wzr.at[k], zp)

    def w_core(k):
        return remote(wbuf.at[k], out_w.at[mine, columns(2 * k + own)], wcs.at[k], wcr.at[k], core)

    def w_local(k):
        return pltpu.make_async_copy(wbuf.at[k], out_w.at[mine, columns(2 * k + own)], wls.at[k])

    def w_forward(k):
        return remote(wrec.at[k], out_w.at[mine, columns(2 * k + 1 - own)], wfs.at[k], wfr.at[k], core)

    def w_keep(k):
        return pltpu.make_async_copy(wrec.at[k], out_w.at[mine, columns(2 * k + 1 - own)], wms.at[k])

    def w_core_wait(k):
        return remote(wbuf.at[k], out_w.at[others, columns(2 * k + own)], wcs.at[k], wcr.at[k], core)

    def w_forward_wait(k):
        return remote(wrec.at[k], out_w.at[others, columns(2 * k + 1 - own)], wfs.at[k], wfr.at[k], core)

    def slot_rows(s):
        return pl.ds(pl.multiple_of(s * ROWS, ROWS), ROWS)

    def put_momentum(s):
        return pltpu.make_async_copy(mom.at[slot_rows(s)], out_momentum.at[slot_rows(s)], osem.at[0, s])

    def put_master(s):
        return pltpu.make_async_copy(mas.at[slot_rows(s)], out_master.at[slot_rows(s)], osem.at[1, s])

    def send_z(j):
        k = chunk(j)
        b = 2 * k + 1 - own
        core_copy(k).wait_recv()
        zbuf[k] = (dec[b, mine, :].astype(F32) + crec[b].astype(F32)).astype(BF16)
        z_copy(k).start()

    def first(j, _):
        k = chunk(j)
        load_levels(j).wait()
        s = pltpu.roll(sc2[...], (128 - 4 * k) % 128, 1)
        for h in range(4):
            lanes = slice(h * BLOCK, (h + 1) * BLOCK)
            to = slice(h % 2 * BLOCK, (h % 2 + 1) * BLOCK)
            dec[2 * k + h // 2, :, to] = (lv[j, :, lanes].astype(F32) * s[:, h:h + 1]).astype(BF16)

        @pl.when((j == 0) & jnp.logical_not(leader))
        def _():
            pl.semaphore_wait(near, 1)

        core_copy(k).start()

        @pl.when(herald & (j < 8))
        def _():
            for i in range(4):
                g = (f + 4 * j + i) % 32

                @pl.when(4 * j + i > 0)
                def _():
                    pl.semaphore_signal(bar, inc=1, device_id=(3, g), device_id_type=MESH)

        @pl.when(j >= LAG)
        def _():
            send_z(j - LAG)
        return 0

    lax.fori_loop(0, 16, first, 0)

    def drain(j, _):
        send_z(j)
        return 0

    lax.fori_loop(16 - LAG, 16, drain, 0)

    load_master().wait()
    load_momentum().wait()

    def make_u(j, _):
        rows = pl.ds(pl.multiple_of(j * ROWS, ROWS), ROWS)
        ubuf[j] = (mas[rows, :] - MOM * mom[rows, :]).astype(BF16)
        return 0

    lax.fori_loop(0, 16, make_u, 0)

    @pl.when(herald)
    def _():
        pl.semaphore_wait(bar, 31)
        for member in (0, 1, 2):
            pl.semaphore_signal(far, inc=1, device_id=(member, f), device_id_type=MESH)

    @pl.when(jnp.logical_not(herald))
    def _():
        pl.semaphore_wait(far, 1)

    def send_relay(i, _):
        relay_copy(i).start()
        return 0

    lax.fori_loop(0, 4, send_relay, 0)

    def send_u(i, _):
        here = same & (i == 0)

        @pl.when(here)
        def _():
            urec[my_chunk] = ubuf[my_slot]

        @pl.when(jnp.logical_not(here))
        def _():
            u_copy(i).start()
        return 0

    lax.fori_loop(0, 8, send_u, 0)

    def send_forward(i, _):
        here = passed & (i == 0)

        @pl.when(i % 2 == 0)
        def _():
            relay_wait(i // 2).wait_recv()

        @pl.when(here)
        def _():
            urec[my_chunk] = rel[y, c]

        @pl.when(jnp.logical_not(here))
        def _():
            forward_copy(i).start()
        return 0

    lax.fori_loop(0, 8, send_forward, 0)

    def whole(j, _):
        k = chunk(j)
        b = 2 * k + own
        here = same & (j == 0)
        z_copy(k).wait_recv()
        gbuf[k] = (dec[b, mine, :].astype(F32) + crec[b].astype(F32) + zrec[k].astype(F32)).astype(BF16)

        @pl.when(here)
        def _():
            grec[my_slot] = gbuf[k]

        @pl.when(jnp.logical_not(here))
        def _():
            g_copy(j).start()

        @pl.when(jnp.logical_not((same | passed) & (j == 0)))
        def _():
            u_wait(k).wait_recv()

        total = dec[b, mine, :].astype(F32) + crec[b].astype(F32) + zrec[k].astype(F32)
        wbuf[k] = (urec[k].astype(F32) - (GRAD / 4) * total).astype(BF16)
        w_z(k).start()
        w_core(k).start()
        w_local(k).start()
        return 0

    lax.fori_loop(0, 16, whole, 0)

    def update(j, _):
        s = row_slot(j)
        rows = slot_rows(s)

        @pl.when(jnp.logical_not(same & (j == 0)))
        def _():
            g_wait(s).wait_recv()

        g = grec[s].astype(F32) * 0.25
        new_momentum = momentum_coef * mom[rows, :] + g
        mom[rows, :] = new_momentum
        mas[rows, :] = mas[rows, :] - outer_rate * (g + momentum_coef * new_momentum)
        put_momentum(s).start()
        put_master(s).start()
        return 0

    lax.fori_loop(0, 16, update, 0)

    def over(j):
        k = chunk(j)
        w_z(k).wait_send()
        w_forward(k).wait_send()
        w_keep(k).wait()
        w_forward_wait(k).wait_recv()

    def pass_on(j, _):
        k = chunk(j)
        core_copy(k).wait_send()
        z_copy(k).wait_send()

        @pl.when(jnp.logical_not(same & (j == 0)))
        def _():
            g_copy(j).wait_send()

        @pl.when((j < 8) & jnp.logical_not(same & (j == 0)))
        def _():
            u_copy(j).wait_send()

        @pl.when((j < 8) & jnp.logical_not(passed & (j == 0)))
        def _():
            forward_copy(j).wait_send()

        @pl.when(j < 4)
        def _():
            relay_copy(j).wait_send()

        put_momentum(j).wait()
        put_master(j).wait()
        w_core(k).wait_send()
        w_local(k).wait()
        w_core_wait(k).wait_recv()

        w_z(k).wait_recv()
        w_forward(k).start()
        w_keep(k).start()

        @pl.when(j >= 4)
        def _():
            over(j - 4)
        return 0

    lax.fori_loop(0, 16, pass_on, 0)

    def finish(j, _):
        over(j)
        return 0

    lax.fori_loop(12, 16, finish, 0)


def per_device(levels, scales, master, momentum):
    small = pltpu.VMEM((CHUNKS, ROWS, COLS), BF16)
    sems = pltpu.SemaphoreType.DMA((16,))
    hbm = pl.BlockSpec(memory_space=pltpu.HBM)
    free = pl.BlockSpec(memory_space=pl.ANY)
    return pl.pallas_call(
        kernel,
        out_shape=(
            jax.ShapeDtypeStruct(master.shape, F32),
            jax.ShapeDtypeStruct(momentum.shape, F32),
            jax.ShapeDtypeStruct(levels.shape[1:], BF16),
        ),
        in_specs=[hbm] * 4,
        out_specs=(free,) * 3,
        scratch_shapes=[
            pltpu.VMEM((CHUNKS, 2 * ROWS, 2 * COLS), jnp.int32),
            pltpu.VMEM((64, 2 * ROWS), F32),
            pltpu.VMEM((2 * ROWS, 128), F32),
            pltpu.VMEM(master.shape, F32),
            pltpu.VMEM(momentum.shape, F32),
            pltpu.VMEM((2 * CHUNKS, 2 * ROWS, COLS), BF16),
            pltpu.VMEM((2 * CHUNKS, ROWS, COLS), BF16),
        ]
        + [small] * 6
        + [pltpu.VMEM((4, 2, ROWS, COLS), BF16)]
        + [small] * 2
        + [pltpu.SemaphoreType.REGULAR] * 2
        + [
            sems,
            pltpu.SemaphoreType.DMA,
            pltpu.SemaphoreType.DMA((2,)),
        ]
        + [sems] * 8
        + [pltpu.SemaphoreType.DMA((4,))] * 2
        + [pltpu.SemaphoreType.DMA((8,))]
        + [sems] * 8
        + [pltpu.SemaphoreType.DMA((2, 16))],
        compiler_params=pltpu.CompilerParams(
            collective_id=0, has_side_effects=True, vmem_limit_bytes=40 * 2**20
        ),
    )(*[
        pltpu.with_memory_space_constraint(a, pltpu.HBM)
        for a in (levels, jnp.swapaxes(scales, 1, 2), master, momentum)
    ])


def solution(mesh):
    in_specs = (
        P("replica", "fsdp", None),
        P("replica", "fsdp", None),
        P("replica", "fsdp"),
        P("replica", "fsdp"),
    )
    out_specs = (P("replica", "fsdp"), P("replica", "fsdp"), P("fsdp", None))
    return jax.shard_map(
        per_device, mesh=mesh, in_specs=in_specs, out_specs=out_specs, check_vma=False
    )
```

time: 78.1 us -> 63.7 us (0.82)
  the two profiles are of different devices: /device:TPU:65 before, /device:TPU:1 now
where the time goes in v2:
time: 63.7 us; the launch traced here: 63.6 us
  Pallas kernels  58.3 us (92%)
  local copies, waits for them, and re-layouts  4.65 us (7%)
  between operations  0.64 us (1%)
    pallas_call x1, Pallas kernels, per_device(): pl.pallas_call(kernel, out_shape=(jax.ShapeDtypeStruct(master.shape, F32)...  58.3 us
    unnamed x3, local copies, waits for them, and re-layouts  4.65 us

profile of v2, /device:TPU:1, one launch (start us, length us, event | category | flops | bytes accessed | tf_op | source)
XLA Modules:
  0.0 63.6 jit_solution(6850360635274280389)
XLA Ops:
  0.6 58.3 %shard_map.67 = (f32[2048,256]{1,0:T(8,128)S(1)}, f32[2048,256]{1,0:T(8,128)S(1)}, bf16[256,8192]{1,0:T(8,128)(2,1)S(1)}) custom-call(s32[1,256,8192]{2,1,0:T(8,128)} %levels.1, f32[1,64,256]{2,1,0:T(8,128)} %bitcast.1, f32[2048,256]{1,0:T(8,128)} %master.1, f32[2048,256]{1,0:T(8,128)} %momentum.1), custom_call_target="tpu_custom_call" | custom-call | tf_op jit(solution)/shard_map/pallas_call | solution.py:380
  58.9 1.3 %copy.10 = f32[2048,256]{1,0:T(8,128)} copy(f32[2048,256]{1,0:T(8,128)S(1)} %get-tuple-element.6) | data formatting | bytes 4194304
  60.2 1.3 %copy.11 = f32[2048,256]{1,0:T(8,128)} copy(f32[2048,256]{1,0:T(8,128)S(1)} %get-tuple-element.7) | data formatting | bytes 4194304
  61.5 2.0 %copy.12 = bf16[256,8192]{1,0:T(8,128)(2,1)} copy(bf16[256,8192]{1,0:T(8,128)(2,1)S(1)} %get-tuple-element.8) | data formatting | bytes 8388608

commit v3 on v2

v3 whole, which is shorter than its diff:
```python
import functools

import jax
import jax.numpy as jnp
from jax import lax
from jax.experimental import pallas as pl
from jax.experimental.pallas import tpu as pltpu
from jax.sharding import PartitionSpec as P

MESH = pl.DeviceIdType.MESH
F32 = jnp.float32
BF16 = jnp.bfloat16

BLOCK = 128
ROWS = 128
COLS = 256
CHUNKS = 16
AHEAD = 8
LAG = 3

outer_rate = 0.7
momentum_coef = 0.9
MOM = outer_rate * momentum_coef * momentum_coef
GRAD = outer_rate * (1.0 + momentum_coef)


def kernel(
    levels, scales, master, momentum,
    out_master, out_momentum, out_w,
    lv, sc, sc2, mas, mom, dec, crec, zbuf, zrec, gbuf, grec, ubuf, urec, rel, wbuf, wrec,
    near, far, lsem, one, crs, zrs, grs, urs, rrs, wzr,
):
    ssem, masem, mosem, css, zss, gss, uss, rss, fss, wzs, wcs, wcr, wfs, wfr, wls, wms = (one.at[i] for i in range(16))
    r = lax.axis_index("replica")
    f = lax.axis_index("fsdp")
    x, y, zh = f // 8, (f // 2) % 4, f % 2
    zl, c = r // 2, r % 2
    core = (zl * 2 + (1 - c), f)
    zp = ((1 - zl) * 2 + c, f)
    cross = (2 * (1 - zl) + c, x * 8 + y * 2 + 1 - zh)
    own = (zl + zh + x // 2) % 2
    same = r == x
    xf = 2 * (1 - zl) + c
    passed = xf == x
    my_slot = (y * 2 + zh) * 2 + c
    my_chunk = x * 4 + y
    herald = r == 3

    def chunk(j):
        b = j % 4
        return ((x + b) % 4) * 4 + (y + j // 4 + b) % 4

    def row_y(i, x_rows):
        return (y + 8 - (x + 4 - x_rows) % 4 - i) % 4

    bar = pltpu.get_barrier_semaphore()
    for member, greeted in ((0, (1, 2)), (1, (0, 2)), (2, (0,)), (3, (2, 1))):

        @pl.when(r == member)
        def _():
            for other in greeted:
                pl.semaphore_signal(bar, inc=1, device_id=(other, f), device_id_type=MESH)

    def load_scales():
        return pltpu.make_async_copy(scales.at[0], sc, ssem)

    def load_levels(j):
        cols = pl.ds(pl.multiple_of(chunk(j) * 2 * COLS, 2 * COLS), 2 * COLS)
        return pltpu.make_async_copy(levels.at[0, :, cols], lv.at[j], lsem.at[j % AHEAD])

    def load_master():
        return pltpu.make_async_copy(master, mas, masem)

    def load_momentum():
        return pltpu.make_async_copy(momentum, mom, mosem)

    load_scales().start()

    def load(j, _):
        load_levels(j).start()
        return 0

    lax.fori_loop(0, AHEAD, load, 0)
    load_master().start()
    load_momentum().start()

    load_scales().wait()
    by_row = jnp.transpose(sc[...])
    sc2[:, :64] = by_row
    sc2[:, 64:] = by_row

    def remote(src, dst, send, recv, device):
        return pltpu.make_async_remote_copy(
            src_ref=src, dst_ref=dst, send_sem=send, recv_sem=recv, device_id=device, device_id_type=MESH
        )

    def wait_bytes(like, sem):
        pltpu.make_async_copy(like, like, sem).wait()

    mine = pl.ds(pl.multiple_of(c * ROWS, ROWS), ROWS)
    others = pl.ds(pl.multiple_of((1 - c) * ROWS, ROWS), ROWS)

    def core_copy(k):
        return remote(dec.at[pl.ds(2 * k, 2), others, :], crec.at[pl.ds(2 * k, 2)], css, crs.at[k], core)

    def z_copy(k):
        return remote(zbuf.at[k], zrec.at[k], zss, zrs.at[k], zp)

    def u_copy(i):
        ys, cs = row_y(i // 2, r), (c + i) % 2
        s = (ys * 2 + zh) * 2 + cs
        return remote(ubuf.at[s], urec.at[my_chunk], uss, urs.at[i // 2], (2 * zl + cs, r * 8 + ys * 2 + zh))

    def relay_copy(i):
        ys = row_y(i, r)
        return remote(ubuf.at[pl.ds((ys * 2 + 1 - zh) * 2, 2)], rel.at[i], rss, rrs.at[i], cross)

    def forward_copy(i):
        ys, cs = row_y(i // 2, xf), (c + i) % 2
        return remote(
            rel.at[i // 2, cs], urec.at[my_chunk], fss, urs.at[i // 2], (2 * zl + cs, xf * 8 + ys * 2 + zh)
        )

    def g_copy(j):
        k = chunk(j)
        return remote(gbuf.at[k], grec.at[my_slot], gss, grs.at[y], (x, k * 2 + own))

    def columns(block):
        return pl.ds(pl.multiple_of(block * COLS, COLS), COLS)

    def w_z(k):
        return remote(wbuf.at[k], wrec.at[k], wzs, wzr.at[k], zp)

    def w_core(k):
        return remote(wbuf.at[k], out_w.at[mine, columns(2 * k + own)], wcs, wcr, core)

    def w_local(k):
        return pltpu.make_async_copy(wbuf.at[k], out_w.at[mine, columns(2 * k + own)], wls)

    def w_forward(k):
        return remote(wrec.at[k], out_w.at[mine, columns(2 * k + 1 - own)], wfs, wfr, core)

    def w_keep(k):
        return pltpu.make_async_copy(wrec.at[k], out_w.at[mine, columns(2 * k + 1 - own)], wms)

    def slot_rows(s):
        return pl.ds(pl.multiple_of(s * ROWS, ROWS), ROWS)

    def send_z(j):
        k = chunk(j)
        b = 2 * k + 1 - own
        core_copy(k).wait_recv()
        zbuf[k] = (dec[b, mine, :].astype(F32) + crec[b].astype(F32)).astype(BF16)
        z_copy(k).start()

    def make_u(s):
        rows = slot_rows(s)
        ubuf[s] = (mas[rows, :] - MOM * mom[rows, :]).astype(BF16)

    def send_u(i, _):
        here = same & (i == 0)

        @pl.when(here)
        def _():
            urec[my_chunk] = ubuf[my_slot]

        @pl.when(jnp.logical_not(here))
        def _():
            u_copy(i).start()
        return 0

    def first(j, _):
        k = chunk(j)
        load_levels(j).wait()

        @pl.when(j < 16 - AHEAD)
        def _():
            load_levels(j + AHEAD).start()

        s = pltpu.roll(sc2[...], (128 - 4 * k) % 128, 1)
        for h in range(4):
            lanes = slice(h * BLOCK, (h + 1) * BLOCK)
            to = slice(h % 2 * BLOCK, (h % 2 + 1) * BLOCK)
            dec[2 * k + h // 2, :, to] = (lv[j, :, lanes].astype(F32) * s[:, h:h + 1]).astype(BF16)

        @pl.when((j == 0) & (r == 2))
        def _():
            pl.semaphore_wait(bar, 3)
            pl.semaphore_signal(near, inc=1, device_id=(3, f), device_id_type=MESH)

        @pl.when((j == 1) & (r < 2))
        def _():
            pl.semaphore_wait(bar, 2)

        @pl.when((j == 1) & herald)
        def _():
            pl.semaphore_wait(near, 1)

        @pl.when(j == 1)
        def _():
            for i in range(1):
                core_copy(chunk(i)).start()

        @pl.when(j >= 1)
        def _():
            core_copy(k).start()

        @pl.when(herald & (j >= 1) & (j < 1 + 4))
        def _():
            for i in range(8):
                n = 8 * (j - 1) + i

                @pl.when(n > 0)
                def _():
                    pl.semaphore_signal(bar, inc=1, device_id=(3, (f + n) % 32), device_id_type=MESH)

        @pl.when(j >= LAG)
        def _():
            send_z(j - LAG)

        @pl.when(j == 3)
        def _():
            load_master().wait()
            load_momentum().wait()

        @pl.when((j >= 3) & (j < 3 + 4))
        def _():
            for i in range(4):
                make_u(4 * (j - 3) + i)

        @pl.when((j == 8) & herald)
        def _():
            pl.semaphore_wait(bar, 31)
            for member in (0, 1, 2):
                pl.semaphore_signal(far, inc=1, device_id=(member, f), device_id_type=MESH)

        @pl.when((j == 8) & jnp.logical_not(herald))
        def _():
            pl.semaphore_wait(far, 1)

        @pl.when(j == 8)
        def _():
            for i in range(4):
                relay_copy(i).start()
            lax.fori_loop(0, 8, send_u, 0)
        return 0

    lax.fori_loop(0, 16, first, 0)

    def drain(j, _):
        send_z(j)
        return 0

    lax.fori_loop(16 - LAG, 16, drain, 0)

    def send_forward(i, _):
        here = passed & (i == 0)

        @pl.when(i % 2 == 0)
        def _():
            relay_copy(i // 2).wait_recv()

        @pl.when(here)
        def _():
            urec[my_chunk] = rel[0, c]

        @pl.when(jnp.logical_not(here))
        def _():
            forward_copy(i).start()
        return 0

    lax.fori_loop(0, 8, send_forward, 0)

    def whole(j, _):
        k = chunk(j)
        b = 2 * k + own
        here = same & (j == 0)
        z_copy(k).wait_recv()
        gbuf[k] = (dec[b, mine, :].astype(F32) + crec[b].astype(F32) + zrec[k].astype(F32)).astype(BF16)

        @pl.when(here)
        def _():
            grec[my_slot] = gbuf[k]

        @pl.when(jnp.logical_not(here))
        def _():
            g_copy(j).start()

        local = (same | passed) & (j == 0)

        @pl.when(local)
        def _():
            wait_bytes(urec.at[pl.ds(0, 3)], urs.at[0])

        @pl.when((j % 4 == 0) & jnp.logical_not(local))
        def _():
            wait_bytes(urec.at[pl.ds(0, 4)], urs.at[j // 4])

        total = dec[b, mine, :].astype(F32) + crec[b].astype(F32) + zrec[k].astype(F32)
        wbuf[k] = (urec[k].astype(F32) - (GRAD / 4) * total).astype(BF16)
        w_z(k).start()
        w_core(k).start()
        w_local(k).start()
        return 0

    lax.fori_loop(0, 16, whole, 0)

    def update(i, _):
        ys = row_y(i, r)
        local = same & (i == 0)

        @pl.when(local)
        def _():
            wait_bytes(grec.at[pl.ds(0, 3)], grs.at[ys])

        @pl.when(jnp.logical_not(local))
        def _():
            wait_bytes(grec.at[pl.ds(0, 4)], grs.at[ys])

        for n in range(4):
            s = ys * 4 + n
            rows = slot_rows(s)
            g = grec[s].astype(F32) * 0.25
            new_momentum = momentum_coef * mom[rows, :] + g
            mom[rows, :] = new_momentum
            mas[rows, :] = mas[rows, :] - outer_rate * (g + momentum_coef * new_momentum)
        rows = pl.ds(pl.multiple_of(ys * 4 * ROWS, ROWS), 4 * ROWS)
        pltpu.make_async_copy(mom.at[rows], out_momentum.at[rows], mosem).start()
        pltpu.make_async_copy(mas.at[rows], out_master.at[rows], masem).start()
        return 0

    lax.fori_loop(0, 4, update, 0)

    def pass_on(j, _):
        k = chunk(j)
        w_z(k).wait_recv()
        w_forward(k).start()
        w_keep(k).start()
        return 0

    lax.fori_loop(0, 16, pass_on, 0)

    wait_bytes(crec, css)
    wait_bytes(zbuf, zss)
    wait_bytes(rel, rss)
    for sem, buf, blocks, less in ((uss, ubuf, 8, same), (fss, ubuf, 8, passed), (gss, gbuf, 16, same)):

        @pl.when(less)
        def _():
            wait_bytes(buf.at[pl.ds(0, blocks - 1)], sem)

        @pl.when(jnp.logical_not(less))
        def _():
            wait_bytes(buf.at[pl.ds(0, blocks)], sem)

    wait_bytes(mom, mosem)
    wait_bytes(mas, masem)
    for sem in (wcs, wls, wcr, wzs, wms, wfs, wfr):
        wait_bytes(wbuf, sem)


def write_kernel(a, b, w, out_a, out_b, out_w, sems):
    copies = [
        pltpu.make_async_copy(a, out_a, sems.at[0]),
        pltpu.make_async_copy(b, out_b, sems.at[1]),
    ]
    copies += [
        pltpu.make_async_copy(w.at[pl.ds(i * 64, 64)], out_w.at[pl.ds(i * 64, 64)], sems.at[2 + i]) for i in range(4)
    ]
    for copy in copies:
        copy.start()
    for copy in copies:
        copy.wait()


def write(*results):
    free = pl.BlockSpec(memory_space=pl.ANY)
    return pl.pallas_call(
        write_kernel,
        out_shape=tuple(jax.ShapeDtypeStruct(a.shape, a.dtype) for a in results),
        in_specs=[free] * 3,
        out_specs=(free,) * 3,
        scratch_shapes=[pltpu.SemaphoreType.DMA((6,))],
        compiler_params=pltpu.CompilerParams(vmem_limit_bytes=1 * 2**20),
    )(*results)


def per_device(levels, scales, master, momentum):
    small = pltpu.VMEM((CHUNKS, ROWS, COLS), BF16)
    free = pl.BlockSpec(memory_space=pl.ANY)
    return write(*pl.pallas_call(
        kernel,
        out_shape=(
            jax.ShapeDtypeStruct(master.shape, F32),
            jax.ShapeDtypeStruct(momentum.shape, F32),
            jax.ShapeDtypeStruct(levels.shape[1:], BF16),
        ),
        in_specs=[pl.BlockSpec(memory_space=pltpu.HBM)] * 4,
        out_specs=(free,) * 3,
        scratch_shapes=[
            pltpu.VMEM((CHUNKS, 2 * ROWS, 2 * COLS), jnp.int32),
            pltpu.VMEM((64, 2 * ROWS), F32),
            pltpu.VMEM((2 * ROWS, 128), F32),
            pltpu.VMEM(master.shape, F32),
            pltpu.VMEM(momentum.shape, F32),
            pltpu.VMEM((2 * CHUNKS, 2 * ROWS, COLS), BF16),
            pltpu.VMEM((2 * CHUNKS, ROWS, COLS), BF16),
        ]
        + [small] * 6
        + [pltpu.VMEM((4, 2, ROWS, COLS), BF16)]
        + [small] * 2
        + [pltpu.SemaphoreType.REGULAR] * 2
        + [pltpu.SemaphoreType.DMA((n,)) for n in (AHEAD, 16, 16, 16, 4, 4, 4, 16)],
        compiler_params=pltpu.CompilerParams(
            collective_id=0, has_side_effects=True, vmem_limit_bytes=40 * 2**20
        ),
    )(*[
        pltpu.with_memory_space_constraint(a, pltpu.HBM)
        for a in (levels, jnp.swapaxes(scales, 1, 2), master, momentum)
    ]))


def solution(mesh):
    in_specs = (
        P("replica", "fsdp", None),
        P("replica", "fsdp", None),
        P("replica", "fsdp"),
        P("replica", "fsdp"),
    )
    out_specs = (P("replica", "fsdp"), P("replica", "fsdp"), P("fsdp", None))
    return jax.shard_map(
        per_device, mesh=mesh, in_specs=in_specs, out_specs=out_specs, check_vma=False
    )
```

time: 63.7 us -> 58.1 us (0.912)
  local copies, waits for them, and re-layouts: 4.65 us -> 0 us
  Pallas kernels: 58.3 us -> 57.3 us
    unnamed x3 -> x0, local copies, waits for them, and re-layouts: 4.65 us -> none
    pallas_call x1, Pallas kernels: 58.3 us -> 54 us  [per_device(): pl.pallas_call(kernel, out_shape=(jax.ShapeDtypeStruct(master.shape, F32)...]
    pallas_call x0 -> x1, Pallas kernels: none -> 3.35 us  [write(): pl.pallas_call(write_kernel, out_shape=tuple((jax.ShapeDtypeStruct(a.shap...]
where the time goes in v3:
time: 58.1 us; the launch traced here: 58 us
  Pallas kernels  57.3 us (99%)
  between operations  0.64 us (1%)
    pallas_call x1, Pallas kernels, per_device(): pl.pallas_call(kernel, out_shape=(jax.ShapeDtypeStruct(master.shape, F32)...  54 us
    pallas_call x1, Pallas kernels, write(): pl.pallas_call(write_kernel, out_shape=tuple((jax.ShapeDtypeStruct(a.shap...  3.35 us

profile of v3, /device:TPU:1, one launch (start us, length us, event | category | flops | bytes accessed | tf_op | source)
XLA Modules:
  0.0 58.0 jit_solution(13244256314828616515)
XLA Ops:
  0.6 54.0 %shard_map.67 = (f32[2048,256]{1,0:T(8,128)S(1)}, f32[2048,256]{1,0:T(8,128)S(1)}, bf16[256,8192]{1,0:T(8,128)(2,1)S(1)}) custom-call(s32[1,256,8192]{2,1,0:T(8,128)} %levels.1, f32[1,64,256]{2,1,0:T(8,128)} %bitcast.1, f32[2048,256]{1,0:T(8,128)} %master.1, f32[2048,256]{1,0:T(8,128)} %momentum.1), custom_call_target="tpu_custom_call" | custom-call | tf_op jit(solution)/shard_map/pallas_call | solution.py:391
  54.6 3.4 %shard_map.68 = (f32[2048,256]{1,0:T(8,128)}, f32[2048,256]{1,0:T(8,128)}, bf16[256,8192]{1,0:T(8,128)(2,1)}) custom-call(f32[2048,256]{1,0:T(8,128)S(1)} %get-tuple-element.6.a, f32[2048,256]{1,0:T(8,128)S(1)} %get-tuple-element.7.b, bf16[256,8192]{1,0:T(8,128)(2,1)S(1)} %get-tuple-element.8.w), custom_call_target="tpu_custom_call" | custom-call | tf_op jit(solution)/shard_map/pallas_call | solution.py:378

commit v4 on v3

--- a/solution.py
+++ b/solution.py
@@ -16,7 +16,7 @@
 COLS = 256
 CHUNKS = 16
 AHEAD = 8
-LAG = 3
+LAG = 2
 
 outer_rate = 0.7
 momentum_coef = 0.9
@@ -44,7 +44,7 @@
     passed = xf == x
     my_slot = (y * 2 + zh) * 2 + c
     my_chunk = x * 4 + y
-    herald = r == 3
+    herald = r == 0
 
     def chunk(j):
         b = j % 4
@@ -54,13 +54,6 @@
         return (y + 8 - (x + 4 - x_rows) % 4 - i) % 4
 
     bar = pltpu.get_barrier_semaphore()
-    for member, greeted in ((0, (1, 2)), (1, (0, 2)), (2, (0,)), (3, (2, 1))):
-
-        @pl.when(r == member)
-        def _():
-            for other in greeted:
-                pl.semaphore_signal(bar, inc=1, device_id=(other, f), device_id_type=MESH)
-
     def load_scales():
         return pltpu.make_async_copy(scales.at[0], sc, ssem)
 
@@ -80,7 +73,16 @@
         load_levels(j).start()
         return 0
 
-    lax.fori_loop(0, AHEAD, load, 0)
+    load_levels(0).start()
+
+    for member, greeted in ((0, (1, 2, 3)), (1, (2, 3)), (2, (1, 3)), (3, (1, 2))):
+
+        @pl.when(r == member)
+        def _():
+            for other in greeted:
+                pl.semaphore_signal(bar, inc=1, device_id=(other, f), device_id_type=MESH)
+
+    lax.fori_loop(1, AHEAD, load, 0)
     load_master().start()
     load_momentum().start()
 
@@ -183,40 +185,32 @@
             to = slice(h % 2 * BLOCK, (h % 2 + 1) * BLOCK)
             dec[2 * k + h // 2, :, to] = (lv[j, :, lanes].astype(F32) * s[:, h:h + 1]).astype(BF16)
 
-        @pl.when((j == 0) & (r == 2))
+        @pl.when((j == 0) & jnp.logical_not(herald))
         def _():
             pl.semaphore_wait(bar, 3)
-            pl.semaphore_signal(near, inc=1, device_id=(3, f), device_id_type=MESH)
-
-        @pl.when((j == 1) & (r < 2))
-        def _():
-            pl.semaphore_wait(bar, 2)
-
-        @pl.when((j == 1) & herald)
+
+        @pl.when((j == 0) & (r == 1))
+        def _():
+            pl.semaphore_signal(near, inc=1, device_id=(0, f), device_id_type=MESH)
+
+        @pl.when((j == 0) & herald)
         def _():
             pl.semaphore_wait(near, 1)
 
-        @pl.when(j == 1)
-        def _():
-            for i in range(1):
-                core_copy(chunk(i)).start()
-
-        @pl.when(j >= 1)
-        def _():
-            core_copy(k).start()
-
-        @pl.when(herald & (j >= 1) & (j < 1 + 4))
-        def _():
-            for i in range(8):
-                n = 8 * (j - 1) + i
+        core_copy(k).start()
+
+        @pl.when(j >= LAG)
+        def _():
+            send_z(j - LAG)
+
+        @pl.when((j >= 1) & (j < 5))
+        def _():
+            for i in range(2):
+                n = 8 * r + 2 * (j - 1) + i
 
                 @pl.when(n > 0)
                 def _():
-                    pl.semaphore_signal(bar, inc=1, device_id=(3, (f + n) % 32), device_id_type=MESH)
-
-        @pl.when(j >= LAG)
-        def _():
-            send_z(j - LAG)
+                    pl.semaphore_signal(bar, inc=1, device_id=(0, (f + n) % 32), device_id_type=MESH)
 
         @pl.when(j == 3)
         def _():
@@ -231,7 +225,7 @@
         @pl.when((j == 8) & herald)
         def _():
             pl.semaphore_wait(bar, 31)
-            for member in (0, 1, 2):
+            for member in (1, 2, 3):
                 pl.semaphore_signal(far, inc=1, device_id=(member, f), device_id_type=MESH)
 
         @pl.when((j == 8) & jnp.logical_not(herald))

time: 58.1 us -> 57.7 us (level)
  no operation moved by 1% of the time
where the time goes in v4:
time: 57.7 us; the launch traced here: 57.5 us
  Pallas kernels  56.9 us (99%)
  between operations  0.64 us (1%)
    pallas_call x1, Pallas kernels, per_device(): pl.pallas_call(kernel, out_shape=(jax.ShapeDtypeStruct(master.shape, F32)...  53.6 us
    pallas_call x1, Pallas kernels, write(): pl.pallas_call(write_kernel, out_shape=tuple((jax.ShapeDtypeStruct(a.shap...  3.35 us

profile of v4, /device:TPU:1, one launch (start us, length us, event | category | flops | bytes accessed | tf_op | source)
XLA Modules:
  0.0 57.5 jit_solution(15003119773301295284)
XLA Ops:
  0.6 53.6 %shard_map.67 = (f32[2048,256]{1,0:T(8,128)S(1)}, f32[2048,256]{1,0:T(8,128)S(1)}, bf16[256,8192]{1,0:T(8,128)(2,1)S(1)}) custom-call(s32[1,256,8192]{2,1,0:T(8,128)} %levels.1, f32[1,64,256]{2,1,0:T(8,128)} %bitcast.1, f32[2048,256]{1,0:T(8,128)} %master.1, f32[2048,256]{1,0:T(8,128)} %momentum.1), custom_call_target="tpu_custom_call" | custom-call | tf_op jit(solution)/shard_map/pallas_call | solution.py:385
  54.2 3.4 %shard_map.68 = (f32[2048,256]{1,0:T(8,128)}, f32[2048,256]{1,0:T(8,128)}, bf16[256,8192]{1,0:T(8,128)(2,1)}) custom-call(f32[2048,256]{1,0:T(8,128)S(1)} %get-tuple-element.6.a, f32[2048,256]{1,0:T(8,128)S(1)} %get-tuple-element.7.b, bf16[256,8192]{1,0:T(8,128)(2,1)S(1)} %get-tuple-element.8.w), custom_call_target="tpu_custom_call" | custom-call | tf_op jit(solution)/shard_map/pallas_call | solution.py:372

commit v5 on v4

--- a/solution.py
+++ b/solution.py
@@ -15,6 +15,7 @@
 ROWS = 128
 COLS = 256
 CHUNKS = 16
+HEAD = 128
 AHEAD = 8
 LAG = 2
 
@@ -27,16 +28,19 @@
 def kernel(
     levels, scales, master, momentum,
     out_master, out_momentum, out_w,
-    lv, sc, sc2, mas, mom, dec, crec, zbuf, zrec, gbuf, grec, ubuf, urec, rel, wbuf, wrec,
+    lv, sc, sc2, mas, mom, dec, crec, zbuf, zrec, gbuf, grec, ubuf, urec, rel, wbuf, wrec, zraw,
     near, far, lsem, one, crs, zrs, grs, urs, rrs, wzr,
 ):
-    ssem, masem, mosem, css, zss, gss, uss, rss, fss, wzs, wcs, wcr, wfs, wfr, wls, wms = (one.at[i] for i in range(16))
+    ssem, masem, mosem, css, zss, gss, uss, rss, fss, wzs, wcs, wcr, wfs, wfr, wls, wms, xss, xrs = (
+        one.at[i] for i in range(18)
+    )
     r = lax.axis_index("replica")
     f = lax.axis_index("fsdp")
     x, y, zh = f // 8, (f // 2) % 4, f % 2
     zl, c = r // 2, r % 2
     core = (zl * 2 + (1 - c), f)
     zp = ((1 - zl) * 2 + c, f)
+    zd = ((1 - zl) * 2 + (1 - c), f)
     cross = (2 * (1 - zl) + c, x * 8 + y * 2 + 1 - zh)
     own = (zl + zh + x // 2) % 2
     same = r == x
@@ -108,6 +112,17 @@
     def z_copy(k):
         return remote(zbuf.at[k], zrec.at[k], zss, zrs.at[k], zp)
 
+    def head_copy(k):
+        b = 2 * k + 1 - own
+        return remote(dec.at[b, mine, pl.ds(0, HEAD)], zrec.at[k, :, pl.ds(0, HEAD)], zss, zrs.at[k], zp)
+
+    def other_head_copy(k):
+        return remote(dec.at[2 * k + 1 - own, others, pl.ds(0, HEAD)], zraw, xss, xrs, zd)
+
+    def rest_copy(k):
+        cols = pl.ds(HEAD, COLS - HEAD)
+        return remote(zbuf.at[k, :, cols], zrec.at[k, :, cols], zss, zrs.at[k], zp)
+
     def u_copy(i):
         ys, cs = row_y(i // 2, r), (c + i) % 2
         s = (ys * 2 + zh) * 2 + cs
@@ -153,7 +168,14 @@
         b = 2 * k + 1 - own
         core_copy(k).wait_recv()
         zbuf[k] = (dec[b, mine, :].astype(F32) + crec[b].astype(F32)).astype(BF16)
-        z_copy(k).start()
+
+        @pl.when(j == 0)
+        def _():
+            rest_copy(k).start()
+
+        @pl.when(j > 0)
+        def _():
+            z_copy(k).start()
 
     def make_u(s):
         rows = slot_rows(s)
@@ -197,6 +219,11 @@
         def _():
             pl.semaphore_wait(near, 1)
 
+        @pl.when(j == 0)
+        def _():
+            head_copy(k).start()
+            other_head_copy(k).start()
+
         core_copy(k).start()
 
         @pl.when(j >= LAG)
@@ -222,17 +249,17 @@
             for i in range(4):
                 make_u(4 * (j - 3) + i)
 
-        @pl.when((j == 8) & herald)
+        @pl.when((j == 12) & herald)
         def _():
             pl.semaphore_wait(bar, 31)
             for member in (1, 2, 3):
                 pl.semaphore_signal(far, inc=1, device_id=(member, f), device_id_type=MESH)
 
-        @pl.when((j == 8) & jnp.logical_not(herald))
+        @pl.when((j == 12) & jnp.logical_not(herald))
         def _():
             pl.semaphore_wait(far, 1)
 
-        @pl.when(j == 8)
+        @pl.when(j == 12)
         def _():
             for i in range(4):
                 relay_copy(i).start()
@@ -270,6 +297,12 @@
         b = 2 * k + own
         here = same & (j == 0)
         z_copy(k).wait_recv()
+
+        @pl.when(j == 0)
+        def _():
+            other_head_copy(k).wait_recv()
+            zrec[k, :, :HEAD] = (zrec[k, :, :HEAD].astype(F32) + zraw[...].astype(F32)).astype(BF16)
+
         gbuf[k] = (dec[b, mine, :].astype(F32) + crec[b].astype(F32) + zrec[k].astype(F32)).astype(BF16)
 
         @pl.when(here)
@@ -336,6 +369,7 @@
 
     wait_bytes(crec, css)
     wait_bytes(zbuf, zss)
+    wait_bytes(zraw, xss)
     wait_bytes(rel, rss)
     for sem, buf, blocks, less in ((uss, ubuf, 8, same), (fss, ubuf, 8, passed), (gss, gbuf, 16, same)):
 
@@ -403,8 +437,9 @@
         + [small] * 6
         + [pltpu.VMEM((4, 2, ROWS, COLS), BF16)]
         + [small] * 2
+        + [pltpu.VMEM((ROWS, HEAD), BF16)]
         + [pltpu.SemaphoreType.REGULAR] * 2
-        + [pltpu.SemaphoreType.DMA((n,)) for n in (AHEAD, 16, 16, 16, 4, 4, 4, 16)],
+        + [pltpu.SemaphoreType.DMA((n,)) for n in (AHEAD, 18, 16, 16, 4, 4, 4, 16)],
         compiler_params=pltpu.CompilerParams(
             collective_id=0, has_side_effects=True, vmem_limit_bytes=40 * 2**20
         ),

time: 57.7 us -> 56.7 us (0.983)
  Pallas kernels: 56.9 us -> 56 us
    pallas_call x1, Pallas kernels: 53.6 us -> 52.6 us  [per_device(): pl.pallas_call(kernel, out_shape=(jax.ShapeDtypeStruct(master.shape, F32)...]
where the time goes in v5:
time: 56.7 us; the launch traced here: 56.6 us
  Pallas kernels  56 us (99%)
  between operations  0.64 us (1%)
    pallas_call x1, Pallas kernels, per_device(): pl.pallas_call(kernel, out_shape=(jax.ShapeDtypeStruct(master.shape, F32)...  52.6 us
    pallas_call x1, Pallas kernels, write(): pl.pallas_call(write_kernel, out_shape=tuple((jax.ShapeDtypeStruct(a.shap...  3.35 us

profile of v5, /device:TPU:1, one launch (start us, length us, event | category | flops | bytes accessed | tf_op | source)
XLA Modules:
  0.0 56.6 jit_solution(3860670875838020953)
XLA Ops:
  0.6 52.6 %shard_map.67 = (f32[2048,256]{1,0:T(8,128)S(1)}, f32[2048,256]{1,0:T(8,128)S(1)}, bf16[256,8192]{1,0:T(8,128)(2,1)S(1)}) custom-call(s32[1,256,8192]{2,1,0:T(8,128)} %levels.1, f32[1,64,256]{2,1,0:T(8,128)} %bitcast.1, f32[2048,256]{1,0:T(8,128)} %master.1, f32[2048,256]{1,0:T(8,128)} %momentum.1), custom_call_target="tpu_custom_call" | custom-call | tf_op jit(solution)/shard_map/pallas_call | solution.py:419
  53.3 3.4 %shard_map.68 = (f32[2048,256]{1,0:T(8,128)}, f32[2048,256]{1,0:T(8,128)}, bf16[256,8192]{1,0:T(8,128)(2,1)}) custom-call(f32[2048,256]{1,0:T(8,128)S(1)} %get-tuple-element.6.a, f32[2048,256]{1,0:T(8,128)S(1)} %get-tuple-element.7.b, bf16[256,8192]{1,0:T(8,128)(2,1)S(1)} %get-tuple-element.8.w), custom_call_target="tpu_custom_call" | custom-call | tf_op jit(solution)/shard_map/pallas_call | solution.py:406

commit v6 on v5

--- a/solution.py
+++ b/solution.py
@@ -16,6 +16,7 @@
 COLS = 256
 CHUNKS = 16
 HEAD = 128
+TAIL = 128
 AHEAD = 8
 LAG = 2
 
@@ -160,6 +161,29 @@
     def w_keep(k):
         return pltpu.make_async_copy(wrec.at[k], out_w.at[mine, columns(2 * k + 1 - own)], wms)
 
+    def last_z(k):
+        return remote(wbuf.at[k, :, pl.ds(0, TAIL)], wrec.at[k, :, pl.ds(0, TAIL)], wzs, wzr.at[k], zp)
+
+    def tail_columns(block):
+        return pl.ds(pl.multiple_of(block * COLS + TAIL, BLOCK), COLS - TAIL)
+
+    def last_direct(k):
+        cols = tail_columns(2 * k + own)
+        return remote(wbuf.at[k, :, pl.ds(TAIL, COLS - TAIL)], out_w.at[mine, cols], wzs, wms, zp)
+
+    def last_other(k):
+        cols = tail_columns(2 * k + own)
+        return remote(wbuf.at[k, :, pl.ds(TAIL, COLS - TAIL)], out_w.at[mine, cols], wfs, wfr, zd)
+
+    def last_columns(k):
+        return pl.ds(pl.multiple_of((2 * k + 1 - own) * COLS, COLS), TAIL)
+
+    def last_forward(k):
+        return remote(wrec.at[k, :, pl.ds(0, TAIL)], out_w.at[mine, last_columns(k)], wfs, wfr, core)
+
+    def last_keep(k):
+        return pltpu.make_async_copy(wrec.at[k, :, pl.ds(0, TAIL)], out_w.at[mine, last_columns(k)], wms)
+
     def slot_rows(s):
         return pl.ds(pl.multiple_of(s * ROWS, ROWS), ROWS)
 
@@ -325,7 +349,17 @@
 
         total = dec[b, mine, :].astype(F32) + crec[b].astype(F32) + zrec[k].astype(F32)
         wbuf[k] = (urec[k].astype(F32) - (GRAD / 4) * total).astype(BF16)
-        w_z(k).start()
+
+        @pl.when(j < 15)
+        def _():
+            w_z(k).start()
+
+        @pl.when(j == 15)
+        def _():
+            last_z(k).start()
+            last_direct(k).start()
+            last_other(k).start()
+
         w_core(k).start()
         w_local(k).start()
         return 0
@@ -365,7 +399,11 @@
         w_keep(k).start()
         return 0
 
-    lax.fori_loop(0, 16, pass_on, 0)
+    lax.fori_loop(0, 15, pass_on, 0)
+    last = chunk(15)
+    last_z(last).wait_recv()
+    last_forward(last).start()
+    last_keep(last).start()
 
     wait_bytes(crec, css)
     wait_bytes(zbuf, zss)

time: 56.7 us -> 56.5 us (level)
  no operation moved by 1% of the time
where the time goes in v6:
time: 56.5 us; the launch traced here: 56.2 us
  Pallas kernels  55.6 us (98%)
  between operations  0.64 us (1%)
    pallas_call x1, Pallas kernels, per_device(): pl.pallas_call(kernel, out_shape=(jax.ShapeDtypeStruct(master.shape, F32)...  52.2 us
    pallas_call x1, Pallas kernels, write(): pl.pallas_call(write_kernel, out_shape=tuple((jax.ShapeDtypeStruct(a.shap...  3.35 us

profile of v6, /device:TPU:1, one launch (start us, length us, event | category | flops | bytes accessed | tf_op | source)
XLA Modules:
  0.0 56.2 jit_solution(7212655744808971636)
XLA Ops:
  0.6 52.2 %shard_map.67 = (f32[2048,256]{1,0:T(8,128)S(1)}, f32[2048,256]{1,0:T(8,128)S(1)}, bf16[256,8192]{1,0:T(8,128)(2,1)S(1)}) custom-call(s32[1,256,8192]{2,1,0:T(8,128)} %levels.1, f32[1,64,256]{2,1,0:T(8,128)} %bitcast.1, f32[2048,256]{1,0:T(8,128)} %master.1, f32[2048,256]{1,0:T(8,128)} %momentum.1), custom_call_target="tpu_custom_call" | custom-call | tf_op jit(solution)/shard_map/pallas_call | solution.py:457
  52.8 3.4 %shard_map.68 = (f32[2048,256]{1,0:T(8,128)}, f32[2048,256]{1,0:T(8,128)}, bf16[256,8192]{1,0:T(8,128)(2,1)}) custom-call(f32[2048,256]{1,0:T(8,128)S(1)} %get-tuple-element.6.a, f32[2048,256]{1,0:T(8,128)S(1)} %get-tuple-element.7.b, bf16[256,8192]{1,0:T(8,128)(2,1)S(1)} %get-tuple-element.8.w), custom_call_target="tpu_custom_call" | custom-call | tf_op jit(solution)/shard_map/pallas_call | solution.py:444
